TPU v7x, 512 devices: a whole 4x4x16 slice. The times are simulated.
512 devices in a mesh: tm: 32 (over z_lo, y, core), rows: 16 (over z_hi, x).
Axes of the slice: x: 4, y: 4, z: 16 (z_hi: 4, z_lo: 4; z = z_hi * 4 + z_lo), core: 2. Of those that a mesh axis runs over, the one named last changes fastest.
Arguments:
- video: bfloat16 [64, 64, 120, 128], P('tm', 'rows'), may hold values from -6 to 6
- norm_gain: bfloat16 [128], replicated, may hold values from 0.099609375 to 1.8984375
- conv_first: bfloat16 [3, 3, 3, 128, 128], replicated, may hold values from -0.109375 to 0.109375
- conv_second: bfloat16 [3, 3, 3, 128, 128], replicated, may hold values from -0.109375 to 0.109375
- attn_gain: bfloat16 [128], replicated, may hold values from 0.099609375 to 1.8984375
- query_weight: bfloat16 [128, 128], replicated, may hold values from -2 to 2
- key_weight: bfloat16 [128, 128], replicated, may hold values from -2 to 2
- value_weight: bfloat16 [128, 128], replicated, may hold values from -0.5 to 0.5
- out_weight: bfloat16 [128, 128], replicated, may hold values from -0.5 to 0.5
Outputs:
- result: bfloat16 [64, 64, 120, 128], P('tm', 'rows')
All inputs are finite; a program needn't handle non-finite values.
Results may differ from a plain program's by a relative error of at most 0.013.
Values may be sent and summed in bfloat16 or wider, within the bound.
A program may use at most 64 MiB of HBM per device.

v0:
```python
import jax
import jax.numpy as jnp
from jax import lax
from jax.sharding import PartitionSpec as P


def shifted(value, axis, steps):
    count = lax.axis_size(axis)
    leading, last = (max(0, -steps), min(count, count - steps))
    return lax.ppermute(value, axis, [(source, source + steps) for source in range(leading, last)])


def with_halo(x, sides, width):
    for axis, dim in sides:
        size, length = (lax.axis_size(axis), x.shape[dim])
        up = [(i, (i + 1) % size) for i in range(size - 1)]
        down = [(j, i) for i, j in up]
        last = lax.slice_in_dim(x, length - width, length, axis=dim)
        leading = lax.slice_in_dim(x, 0, width, axis=dim)
        before = lax.ppermute(last, axis, up)
        after = lax.ppermute(leading, axis, down)
        x = jnp.concatenate([before, x, after], axis=dim)
    return x


def rms_norm(values, gain):
    wide = values.astype(jnp.float32)
    scale = lax.rsqrt(jnp.mean(wide * wide, axis=-1, keepdims=True) + 1e-06)
    return wide * scale * gain.astype(jnp.float32)


def convolve(field, kernel):
    frames, height, width, chans = field.shape
    earlier = shifted(field, "tm", 1)
    extended = jnp.concatenate([earlier, field], axis=0)
    padded = with_halo(extended, (("rows", 1),), 1)
    padded = jnp.pad(padded, ((0, 0), (0, 0), (1, 1), (0, 0)))
    total = jnp.zeros((frames * height * width, chans), jnp.float32)
    for shift_t in range(3):
        for shift_h in range(3):
            slab = padded[shift_t : shift_t + frames, shift_h : shift_h + height]
            joined = jnp.concatenate([slab[:, :, e : e + width] for e in range(3)], axis=-1)
            taps = kernel[shift_t, shift_h].reshape(3 * chans, chans)
            total = total + jnp.dot(
                joined.reshape(-1, 3 * chans), taps, preferred_element_type=jnp.float32
            )
    return total.reshape(frames, height, width, chans)


def block_scores(query, keys, query_first):
    chans = query.shape[-1]
    scores = jnp.einsum("fpc,gpc->fgp", query, keys, preferred_element_type=jnp.float32) / jnp.sqrt(
        jnp.float32(chans)
    )
    query_pos = query_first + jnp.arange(query.shape[0], dtype=jnp.int32)
    key_pos = jnp.arange(keys.shape[0], dtype=jnp.int32)
    allowed = (key_pos[None, :] <= query_pos[:, None])[:, :, None]
    tile_top = jnp.max(jnp.where(allowed, scores, jnp.float32(-1e30)), axis=1)
    return (scores, allowed, tile_top)


def absorb_block(carry, query, keys, values, query_first):
    top, total, acc = carry
    scores, allowed, tile_top = block_scores(query, keys, query_first)
    new_top = jnp.maximum(top, tile_top)
    weights = jnp.where(allowed, jnp.exp(scores - new_top[:, None, :]), jnp.float32(0.0))
    total = jnp.sum(weights, axis=1)
    update = jnp.einsum(
        "fgp,gpc->fpc", weights.astype(jnp.bfloat16), values, preferred_element_type=jnp.float32
    )
    acc = update
    return (new_top, total, acc)


def start_carry(frames, cells, chans):
    return (
        jnp.full((frames, cells), -1e30, jnp.float32),
        jnp.zeros((frames, cells), jnp.float32),
        jnp.zeros((frames, cells, chans), jnp.float32),
    )


def local(
    video,
    norm_gain,
    conv_first,
    conv_second,
    attn_gain,
    query_weight,
    key_weight,
    value_weight,
    out_weight,
):
    frames, height, width, chans = video.shape
    act = jax.nn.silu(rms_norm(video, norm_gain)).astype(jnp.bfloat16)
    mid = jax.nn.silu(convolve(act, conv_first)).astype(jnp.bfloat16)
    hidden = (video.astype(jnp.float32) + convolve(mid, conv_second)).astype(jnp.bfloat16)
    normed = rms_norm(hidden, attn_gain).astype(jnp.bfloat16)
    flat = normed.reshape(-1, chans)
    joined_weight = jnp.concatenate([query_weight, key_weight, value_weight], axis=1)
    projected = jnp.dot(flat, joined_weight, preferred_element_type=jnp.float32).astype(
        jnp.bfloat16
    )
    cells = height * width
    query = projected[:, :chans].reshape(frames, cells, chans)
    keys = projected[:, chans : 2 * chans].reshape(frames, cells, chans)
    values = projected[:, 2 * chans :].reshape(frames, cells, chans)
    query_first = lax.axis_index("tm") * frames
    top, total, acc = absorb_block(
        start_carry(frames, cells, chans),
        query,
        lax.all_gather(keys, "tm", axis=0, tiled=True),
        lax.all_gather(values, "tm", axis=0, tiled=True),
        query_first,
    )
    mixed = (acc / total[:, :, None]).astype(jnp.bfloat16)
    output = jnp.dot(mixed.reshape(-1, chans), out_weight, preferred_element_type=jnp.float32)
    result = hidden.reshape(-1, chans).astype(jnp.float32) + output
    return result.astype(jnp.bfloat16).reshape(frames, height, width, chans)


def solution(mesh):
    return jax.shard_map(
        local,
        mesh=mesh,
        in_specs=(P("tm", "rows", None, None), P(), P(), P(), P(), P(), P(), P(), P()),
        out_specs=P("tm", "rows", None, None),
        check_vma=False,
    )
```

profile of v0, /device:TPU:1, one launch (start us, length us, event | category | flops | bytes accessed | tf_op | source)
XLA Modules:
  0.0 247.9 jit_solution(13265334246154741844)
XLA Ops:
  6.5 1.2 fusion.26
  7.8 0.7 convert_element_type.47
  8.5 1.2 fusion.33
  9.6 4.6 %collective-permute-start = (bf16[2,4,120,128]{3,2,1,0:T(8,128)(2,1)S(1)}, bf16[2,4,120,128]{3,2,1,0:T(8,128)(2,1)S(1)}, u32[]{:S(2)}, u32[]{:S(2)}) collective-permute-start(bf16[2,4,120,128]{3,2,1,0:T(8,128)(2,1)S(1)} %fusion.33), channel_id=1, source_target_pairs={{0,16},{16,32},{32,48},{48,64},{64,80},{80,96},{96,112},{112,128},... | collective-permute-start | bytes 737288 | tf_op jit(solution)/shard_map/ppermute | solution.py:10
  14.2 4.6 %collective-permute-done = bf16[2,4,120,128]{3,2,1,0:T(8,128)(2,1)S(1)} collective-permute-done((bf16[2,4,120,128]{3,2,1,0:T(8,128)(2,1)S(1)}, bf16[2,4,120,128]{3,2,1,0:T(8,128)(2,1)S(1)}, u32[]{:S(2)}, u32[]{:S(2)}) %collective-permute-start) | collective-permute-done | bytes 245792 | tf_op jit(solution)/shard_map/ppermute | solution.py:10
  18.8 1.7 collective-permute-start.1
  20.5 1.3 collective-permute-start.2
  21.9 1.7 collective-permute-done.1
  23.6 3.9 %collective-permute-done.2 = bf16[4,1,120,128]{3,2,1,0:T(8,128)(2,1)S(1)} collective-permute-done((bf16[4,1,120,128]{3,2,1,0:T(8,128)(2,1)S(1)}, bf16[4,1,120,128]{3,2,1,0:T(8,128)(2,1)S(1)}, u32[]{:S(2)}, u32[]{:S(2)}) %collective-permute-start.2) | collective-permute-done | bytes 122912 | tf_op jit(solution)/shard_map/ppermute | solution.py:21
  27.5 0.3 fusion.19
  27.8 0.6 fusion.51
  28.9 0.3 fusion.57
  29.3 0.4 pad_maximum_fusion.8
  29.7 0.4 convolution_add_fusion.16
  30.0 0.4 convolution_add_fusion.15
  30.6 0.4 convolution_add_fusion.14
  31.0 0.4 convolution_add_fusion.13
  31.3 0.4 convolution_add_fusion.12
  31.7 0.4 convolution_add_fusion.11
  32.1 0.4 convolution_add_fusion.10
  32.5 0.4 convolution_add_fusion.9
  33.1 4.4 %collective-permute-start.3 = (bf16[2,4,120,128]{3,2,1,0:T(8,128)(2,1)S(1)}, bf16[2,4,120,128]{3,2,1,0:T(8,128)(2,1)S(1)}, u32[]{:S(2)}, u32[]{:S(2)}) collective-permute-start(bf16[2,4,120,128]{3,2,1,0:T(8,128)(2,1)S(1)} %multiply_convert_fusion.1), channel_id=1, source_target_pairs={{0,16},{16,32},{32,48},{48,64},{64,80},{80,96},{96,112},{112,128},... | collective-permute-start | bytes 737288 | tf_op jit(solution)/shard_map/ppermute | solution.py:10
  37.5 3.1 %collective-permute-done.3 = bf16[2,4,120,128]{3,2,1,0:T(8,128)(2,1)S(1)} collective-permute-done((bf16[2,4,120,128]{3,2,1,0:T(8,128)(2,1)S(1)}, bf16[2,4,120,128]{3,2,1,0:T(8,128)(2,1)S(1)}, u32[]{:S(2)}, u32[]{:S(2)}) %collective-permute-start.3) | collective-permute-done | bytes 245792 | tf_op jit(solution)/shard_map/ppermute | solution.py:10
  40.6 3.1 %collective-permute-start.4 = (bf16[4,1,120,128]{3,2,1,0:T(8,128)(2,1)S(1)}, bf16[4,1,120,128]{3,2,1,0:T(8,128)(2,1)S(1)}, u32[]{:S(2)}, u32[]{:S(2)}) collective-permute-start(bf16[4,1,120,128]{3,2,1,0:T(8,128)(2,1)S(1)} %get-tuple-element.78), channel_id=1, source_target_pairs={{0,1},{1,2},{2,3},{3,4},{4,5},{5,6},{6,7},{7,8},{8,9},{9,10},{10,1... | collective-permute-start | bytes 368648 | tf_op jit(solution)/shard_map/ppermute | solution.py:20
  43.8 1.3 collective-permute-start.5
  45.2 0.4 collective-permute-done.4
  45.6 8.3 %collective-permute-done.5 = bf16[4,1,120,128]{3,2,1,0:T(8,128)(2,1)S(1)} collective-permute-done((bf16[4,1,120,128]{3,2,1,0:T(8,128)(2,1)S(1)}, bf16[4,1,120,128]{3,2,1,0:T(8,128)(2,1)S(1)}, u32[]{:S(2)}, u32[]{:S(2)}) %collective-permute-start.5) | collective-permute-done | bytes 122912 | tf_op jit(solution)/shard_map/ppermute | solution.py:21
  54.2 0.3 select_maximum_fusion
  54.5 0.6 fusion.50
  55.3 0.4 fusion.58
  56.2 0.3 pad_maximum_fusion.16
  56.5 0.4 convolution_add_fusion.8
  56.8 0.4 convolution_add_fusion.7
  57.2 0.4 convolution_add_fusion.6
  57.5 0.4 convolution_add_fusion.5
  57.9 0.4 convolution_add_fusion.4
  58.3 0.4 convolution_add_fusion.3
  58.6 0.4 convolution_add_fusion.2
  59.0 0.4 convolution_add_fusion.1
  60.0 0.3 convolution_convert_fusion
  60.4 0.9 fusion.52
  61.6 0.5 all-gather.3.cloned.1.call-update
  62.2 96.7 %all-gather.5.cloned.1.call-done = bf16[64,480,128]{2,1,0:T(8,128)(2,1)} async-done(((bf16[2,480,128]{2,1,0:T(8,128)(2,1)}), bf16[64,480,128]{2,1,0:T(8,128)(2,1)}) %all-gather.5.cloned.1.call-update) | async-done | bytes 7864336 | tf_op jit(solution)/shard_map/all_gather | solution.py:112
  158.9 7.5 %select_reduce_fusion = (f32[2,480]{0,1:T(8,128)S(1)}, f32[2,64,480]{1,0,2:T(2,128)S(1)}) fusion(pred[2,64]{1,0:T(4,128)(4,1)S(1)} %iota_compare_fusion.2, bf16[2,480,128]{2,1,0:T(8,128)(2,1)S(1)} %bitcast.133, bf16[64,480,128]{2,1,0:T(8,128)(2,1)} %all-gather.5.cloned.1.call-done), kind=kOutput, calls=%fused_computation.81 | convolution fusion | flops 15912000 | bytes 8359808 | tf_op jit(solution)/shard_map/fpc,gpc->fgp/dot_general | solution.py:52
  166.5 1.5 fusion.44
  168.1 65.8 %all-gather.3.cloned.1.call-done = bf16[64,480,128]{2,1,0:T(8,128)(2,1)} async-done(((bf16[2,480,128]{2,1,0:T(8,128)(2,1)}), bf16[64,480,128]{2,1,0:T(8,128)(2,1)}) %all-gather.3.cloned.1.call-update) | async-done | bytes 7864336 | tf_op jit(solution)/shard_map/all_gather | solution.py:113
  233.9 6.1 %fusion = f32[480,128,2]{1,2,0:T(2,128)S(1)} fusion(bf16[64,480,128]{2,1,0:T(8,128)(2,1)} %all-gather.3.cloned.1.call-done, f32[2,64,480]{1,0,2:T(2,128)S(1)} %get-tuple-element.91, pred[2,64]{1,0:T(4,128)(4,1)S(1)} %iota_compare_fusion.2, f32[2,480]{0,1:T(8,128)S(1)} %broadcast_maximum_fusion), kind=kOutput, calls=%fused_computation | convolution fusion | flops 15912960 | bytes 8605568 | tf_op jit(solution)/shard_map/fgp,gpc->fpc/dot_general | solution.py:68
  240.2 0.9 fusion.5
  (49 shorter events, 3.4 us)
Async XLA Ops:
  6.5 233.6 %copy-start = (bf16[128,128]{1,0:T(8,128)(2,1)S(1)}, bf16[128,128]{1,0:T(8,128)(2,1)}, u32[]{:S(2)}) copy-start(bf16[128,128]{1,0:T(8,128)(2,1)} %param.17) | copy-start | bytes 98308
  6.5 15.3 %copy-start.2 = (bf16[3,3,3,128,128]{4,3,2,1,0:T(8,128)(2,1)S(1)}, bf16[3,3,3,128,128]{4,3,2,1,0:T(8,128)(2,1)}, u32[]{:S(2)}) copy-start(bf16[3,3,3,128,128]{4,3,2,1,0:T(8,128)(2,1)} %param.11) | copy-start | bytes 2654212
  6.5 152.4 %all-gather.5.cloned.1.call-start = ((), (), s32[]{:S(2)}) async-start(), calls=%async_computation.1 | async-start | bytes 8110080 | tf_op jit(solution)/shard_map/all_gather | solution.py:112
  9.6 9.2 %collective-permute-start = (bf16[2,4,120,128]{3,2,1,0:T(8,128)(2,1)S(1)}, bf16[2,4,120,128]{3,2,1,0:T(8,128)(2,1)S(1)}, u32[]{:S(2)}, u32[]{:S(2)}) collective-permute-start(bf16[2,4,120,128]{3,2,1,0:T(8,128)(2,1)S(1)} %fusion.33), channel_id=1, source_target_pairs={{0,16},{16,32},{32,48},{48,64},{64,80},{80,96},{96,112},{112,128},... | collective-permute-start | bytes 737288 | tf_op jit(solution)/shard_map/ppermute | solution.py:10
  18.8 4.8 %collective-permute-start.1 = (bf16[4,1,120,128]{3,2,1,0:T(8,128)(2,1)S(1)}, bf16[4,1,120,128]{3,2,1,0:T(8,128)(2,1)S(1)}, u32[]{:S(2)}, u32[]{:S(2)}) collective-permute-start(bf16[4,1,120,128]{3,2,1,0:T(8,128)(2,1)S(1)} %get-tuple-element.82), channel_id=1, source_target_pairs={{0,1},{1,2},{2,3},{3,4},{4,5},{5,6},{6,7},{7,8},{8,9},{9,10},{10,1... | collective-permute-start | bytes 368648 | tf_op jit(solution)/shard_map/ppermute | solution.py:20
  20.5 7.0 %collective-permute-start.2 = (bf16[4,1,120,128]{3,2,1,0:T(8,128)(2,1)S(1)}, bf16[4,1,120,128]{3,2,1,0:T(8,128)(2,1)S(1)}, u32[]{:S(2)}, u32[]{:S(2)}) collective-permute-start(bf16[4,1,120,128]{3,2,1,0:T(8,128)(2,1)S(1)} %get-tuple-element.83), channel_id=1, source_target_pairs={{1,0},{2,1},{3,2},{4,3},{5,4},{6,5},{7,6},{8,7},{9,8},{10,9},{11,1... | collective-permute-start | bytes 368648 | tf_op jit(solution)/shard_map/ppermute | solution.py:21
  32.5 12.5 %copy-start.3 = (bf16[3,3,3,128,128]{4,3,2,1,0:T(8,128)(2,1)S(1)}, bf16[3,3,3,128,128]{4,3,2,1,0:T(8,128)(2,1)}, u32[]{:S(2)}) copy-start(bf16[3,3,3,128,128]{4,3,2,1,0:T(8,128)(2,1)} %param.12) | copy-start | bytes 2654212
  32.9 12.3 %copy-start.7 = (bf16[128]{0:T(256)(128)(2,1)S(1)}, bf16[128]{0:T(256)(128)(2,1)}, u32[]{:S(2)}) copy-start(bf16[128]{0:T(256)(128)(2,1)} %param.13) | copy-start | bytes 772
  33.1 7.5 %collective-permute-start.3 = (bf16[2,4,120,128]{3,2,1,0:T(8,128)(2,1)S(1)}, bf16[2,4,120,128]{3,2,1,0:T(8,128)(2,1)S(1)}, u32[]{:S(2)}, u32[]{:S(2)}) collective-permute-start(bf16[2,4,120,128]{3,2,1,0:T(8,128)(2,1)S(1)} %multiply_convert_fusion.1), channel_id=1, source_target_pairs={{0,16},{16,32},{32,48},{48,64},{64,80},{80,96},{96,112},{112,128},... | collective-permute-start | bytes 737288 | tf_op jit(solution)/shard_map/ppermute | solution.py:10
  40.6 5.0 %collective-permute-start.4 = (bf16[4,1,120,128]{3,2,1,0:T(8,128)(2,1)S(1)}, bf16[4,1,120,128]{3,2,1,0:T(8,128)(2,1)S(1)}, u32[]{:S(2)}, u32[]{:S(2)}) collective-permute-start(bf16[4,1,120,128]{3,2,1,0:T(8,128)(2,1)S(1)} %get-tuple-element.78), channel_id=1, source_target_pairs={{0,1},{1,2},{2,3},{3,4},{4,5},{5,6},{6,7},{7,8},{8,9},{9,10},{10,1... | collective-permute-start | bytes 368648 | tf_op jit(solution)/shard_map/ppermute | solution.py:20
  43.8 10.2 %collective-permute-start.5 = (bf16[4,1,120,128]{3,2,1,0:T(8,128)(2,1)S(1)}, bf16[4,1,120,128]{3,2,1,0:T(8,128)(2,1)S(1)}, u32[]{:S(2)}, u32[]{:S(2)}) collective-permute-start(bf16[4,1,120,128]{3,2,1,0:T(8,128)(2,1)S(1)} %get-tuple-element.79), channel_id=1, source_target_pairs={{1,0},{2,1},{3,2},{4,3},{5,4},{6,5},{7,6},{8,7},{9,8},{10,9},{11,1... | collective-permute-start | bytes 368648 | tf_op jit(solution)/shard_map/ppermute | solution.py:21
  58.6 0.9 copy-start.1
  59.0 1.0 copy-start.4
  59.0 1.0 copy-start.5
  59.0 1.0 copy-start.6
  61.3 172.5 %all-gather.3.cloned.1.call-start = ((), (), s32[]{:S(2)}) async-start(), calls=%async_computation | async-start | bytes 8110080 | tf_op jit(solution)/shard_map/all_gather | solution.py:113
Sparse Core Ops, SparseCore 0:
  61.4 97.4 all-gather.4
  161.1 72.7 all-gather.2
where the time goes:
time: 248 us
  waiting for transfers between devices  185 us (75%)
  matrix products  21.2 us (9%)
  starting transfers between devices  16.6 us (7%)
  between operations  14 us (6%)
  other arithmetic  8.13 us (3%)
  local copies, waits for them, and re-layouts  2.88 us (1%)
    all_gather x1, waiting for transfers between devices, local(): lax.all_gather(keys, 'tm', axis=0, tiled=True)  96.7 us
    all_gather x1, waiting for transfers between devices, local(): lax.all_gather(values, 'tm', axis=0, tiled=True)  65.8 us
    ppermute x2, waiting for transfers between devices, with_halo(): after = lax.ppermute(leading, axis, down)  12.2 us
    ppermute x2, starting transfers between devices, shifted(): lax.ppermute(value, axis, [(source, source + steps) for source in range(l...  9.02 us
    ppermute x2, waiting for transfers between devices, shifted(): lax.ppermute(value, axis, [(source, source + steps) for source in range(l...  7.68 us
    dot_general x1, matrix products, block_scores(): jnp.einsum('fpc,gpc->fgp', query, keys, preferred_element_type=jnp.float32)  7.5 us
    dot_general x18, matrix products, convolve(): jnp.dot(joined.reshape(-1, 3 * chans), taps, preferred_element_type=jnp.f...  6.36 us
    dot_general x1, matrix products, absorb_block(): jnp.einsum('fgp,gpc->fpc', weights.astype(jnp.bfloat16), values, preferre...  6.08 us
  transfers between devices with their start and end apart: 8, of which 8 were waited for; matrix products, arithmetic and copies ran while one was open for 4% of the time, Pallas kernels for 0%

commit v1 on v0

--- a/solution.py
+++ b/solution.py
@@ -2,6 +2,13 @@
 import jax.numpy as jnp
 from jax import lax
 from jax.sharding import PartitionSpec as P
+
+
+def exchange_gather(shard, mesh_axis, along):
+    devices = lax.axis_size(mesh_axis)
+    blocks = jnp.stack([shard for _ in range(devices)])
+    blocks = lax.all_to_all(blocks, mesh_axis, split_axis=0, concat_axis=0)
+    return jnp.concatenate(blocks, axis=along)
 
 
 def shifted(value, axis, steps):
@@ -110,7 +117,7 @@
         start_carry(frames, cells, chans),
         query,
         lax.all_gather(keys, "tm", axis=0, tiled=True),
-        lax.all_gather(values, "tm", axis=0, tiled=True),
+        exchange_gather(values, "tm", 0),
         query_first,
     )
     mixed = (acc / total[:, :, None]).astype(jnp.bfloat16)

time: 248 us -> 334 us (1.35)
  the two profiles are of different devices: /device:TPU:1 before, /device:TPU:6 now
where the time goes in v1:
time: 334 us
  waiting for transfers between devices  225 us (67%)
  starting transfers between devices  49 us (15%)
  local copies, waits for them, and re-layouts  20.7 us (6%)
  matrix products  17.3 us (5%)
  between operations  14 us (4%)
  other arithmetic  8.13 us (2%)
    all_gather x1, waiting for transfers between devices, local(): lax.all_gather(keys, 'tm', axis=0, tiled=True)  176 us
    all_to_all x1, starting transfers between devices, exchange_gather(): blocks = lax.all_to_all(blocks, mesh_axis, split_axis=0, concat_axis=0)  26.1 us
    all_to_all x1, waiting for transfers between devices, exchange_gather(): blocks = lax.all_to_all(blocks, mesh_axis, split_axis=0, concat_axis=0)  25.9 us
    ppermute x2, waiting for transfers between devices, with_halo(): after = lax.ppermute(leading, axis, down)  18.3 us
    ppermute x2, starting transfers between devices, with_halo(): before = lax.ppermute(last, axis, up)  10.9 us
    all_to_all x1, local copies, waits for them, and re-layouts, exchange_gather(): blocks = lax.all_to_all(blocks, mesh_axis, split_axis=0, concat_axis=0)  9.54 us
    another operation x2, local copies, waits for them, and re-layouts, exchange_gather(): blocks = jnp.stack([shard for _ in range(devices)])  8.38 us
    dot_general x1, matrix products, block_scores(): jnp.einsum('fpc,gpc->fgp', query, keys, preferred_element_type=jnp.float32)  7.5 us
  transfers between devices with their start and end apart: 8, of which 8 were waited for; matrix products, arithmetic and copies ran while one was open for 3% of the time, Pallas kernels for 0%

profile of v1, /device:TPU:6, one launch (start us, length us, event | category | flops | bytes accessed | tf_op | source)
XLA Modules:
  0.0 333.8 jit_solution(18140199567241157185)
XLA Ops:
  6.5 0.7 convert_element_type.47
  7.3 1.2 fusion.24
  8.5 1.2 fusion.31
  9.6 1.8 collective-permute-start
  11.4 1.1 collective-permute-done
  12.5 9.0 %collective-permute-start.1 = (bf16[4,1,120,128]{3,2,1,0:T(8,128)(2,1)S(1)}, bf16[4,1,120,128]{3,2,1,0:T(8,128)(2,1)S(1)}, u32[]{:S(2)}, u32[]{:S(2)}) collective-permute-start(bf16[4,1,120,128]{3,2,1,0:T(8,128)(2,1)S(1)} %get-tuple-element.82), channel_id=1, source_target_pairs={{0,1},{1,2},{2,3},{3,4},{4,5},{5,6},{6,7},{7,8},{8,9},{9,10},{10,1... | collective-permute-start | bytes 368648 | tf_op jit(solution)/shard_map/ppermute | solution.py:27
  21.5 1.9 collective-permute-start.2
  23.6 0.4 collective-permute-done.1
  24.0 10.4 %collective-permute-done.2 = bf16[4,1,120,128]{3,2,1,0:T(8,128)(2,1)S(1)} collective-permute-done((bf16[4,1,120,128]{3,2,1,0:T(8,128)(2,1)S(1)}, bf16[4,1,120,128]{3,2,1,0:T(8,128)(2,1)S(1)}, u32[]{:S(2)}, u32[]{:S(2)}) %collective-permute-start.2) | collective-permute-done | bytes 122912 | tf_op jit(solution)/shard_map/ppermute | solution.py:28
  35.0 0.6 fusion.50
  35.8 0.4 fusion.56
  36.2 0.4 pad_maximum_fusion.8
  36.6 0.4 convolution_add_fusion.16
  37.0 0.4 convolution_add_fusion.15
  37.5 0.4 convolution_add_fusion.14
  37.9 0.4 convolution_add_fusion.13
  38.2 0.4 convolution_add_fusion.12
  38.6 0.4 convolution_add_fusion.11
  39.0 0.4 convolution_add_fusion.10
  39.3 0.4 convolution_add_fusion.9
  39.9 4.3 %collective-permute-start.3 = (bf16[2,4,120,128]{3,2,1,0:T(8,128)(2,1)S(1)}, bf16[2,4,120,128]{3,2,1,0:T(8,128)(2,1)S(1)}, u32[]{:S(2)}, u32[]{:S(2)}) collective-permute-start(bf16[2,4,120,128]{3,2,1,0:T(8,128)(2,1)S(1)} %multiply_convert_fusion.1), channel_id=1, source_target_pairs={{0,16},{16,32},{32,48},{48,64},{64,80},{80,96},{96,112},{112,128},... | collective-permute-start | bytes 737288 | tf_op jit(solution)/shard_map/ppermute | solution.py:17
  44.2 1.1 collective-permute-done.3
  45.4 1.9 collective-permute-start.4
  47.3 3.9 %collective-permute-start.5 = (bf16[4,1,120,128]{3,2,1,0:T(8,128)(2,1)S(1)}, bf16[4,1,120,128]{3,2,1,0:T(8,128)(2,1)S(1)}, u32[]{:S(2)}, u32[]{:S(2)}) collective-permute-start(bf16[4,1,120,128]{3,2,1,0:T(8,128)(2,1)S(1)} %get-tuple-element.79), channel_id=1, source_target_pairs={{1,0},{2,1},{3,2},{4,3},{5,4},{6,5},{7,6},{8,7},{9,8},{10,9},{11,1... | collective-permute-start | bytes 368648 | tf_op jit(solution)/shard_map/ppermute | solution.py:28
  51.3 0.8 collective-permute-done.4
  52.1 7.9 %collective-permute-done.5 = bf16[4,1,120,128]{3,2,1,0:T(8,128)(2,1)S(1)} collective-permute-done((bf16[4,1,120,128]{3,2,1,0:T(8,128)(2,1)S(1)}, bf16[4,1,120,128]{3,2,1,0:T(8,128)(2,1)S(1)}, u32[]{:S(2)}, u32[]{:S(2)}) %collective-permute-start.5) | collective-permute-done | bytes 122912 | tf_op jit(solution)/shard_map/ppermute | solution.py:28
  60.7 0.6 fusion.49
  61.4 0.3 fusion.57
  62.6 0.4 convolution_add_fusion.8
  62.9 0.4 convolution_add_fusion.7
  63.3 0.4 convolution_add_fusion.6
  63.7 0.4 convolution_add_fusion.5
  64.0 0.4 convolution_add_fusion.4
  64.4 0.4 convolution_add_fusion.3
  64.8 0.4 convolution_add_fusion.2
  65.2 0.4 convolution_add_fusion.1
  66.2 0.3 convolution_convert_fusion
  66.5 0.8 fusion.51
  67.5 8.2 %stack.3 = bf16[32,2,480,128]{3,1,2,0:T(2,128)(2,1)} broadcast(bf16[2,480,128]{2,0,1:T(2,128)(2,1)S(1)} %copy.27), dimensions={1,2,3} | broadcast | bytes 8110080 | tf_op jit(solution)/shard_map/stack | solution.py:9
  75.7 26.1 %all-to-all-start = ((bf16[32,2,480,128]{3,1,2,0:T(2,128)(2,1)}), bf16[32,2,480,128]{3,1,2,0:T(2,128)(2,1)}, u32[]{:S(2)}, u32[]{:S(2)}) async-start(bf16[32,2,480,128]{3,1,2,0:T(2,128)(2,1)} %stack.3), calls=%async_computation | async-start | bytes 15728640 | tf_op jit(solution)/shard_map/all_to_all | solution.py:10
  101.9 0.7 all-gather.2.cloned.1.call-update
  102.7 176.3 %all-gather.2.cloned.1.call-done = bf16[64,480,128]{2,1,0:T(8,128)(2,1)} async-done(((bf16[2,480,128]{2,1,0:T(8,128)(2,1)}), bf16[64,480,128]{2,1,0:T(8,128)(2,1)}) %all-gather.2.cloned.1.call-update) | async-done | bytes 7864336 | tf_op jit(solution)/shard_map/all_gather | solution.py:119
  279.0 7.5 %select_reduce_fusion = (f32[2,480]{0,1:T(8,128)S(1)}, f32[2,64,480]{1,0,2:T(2,128)S(1)}) fusion(pred[2,64]{1,0:T(4,128)(4,1)S(1)} %iota_compare_fusion.2, bf16[2,480,128]{2,1,0:T(8,128)(2,1)S(1)} %bitcast.136, bf16[64,480,128]{2,1,0:T(8,128)(2,1)} %all-gather.2.cloned.1.call-done), kind=kOutput, calls=%fused_computation.79 | convolution fusion | flops 15912000 | bytes 8359808 | tf_op jit(solution)/shard_map/fpc,gpc->fgp/dot_general | solution.py:59
  286.5 1.5 fusion.43
  288.2 25.9 %all-to-all-done = bf16[32,2,480,128]{3,1,2,0:T(2,128)(2,1)} async-done(((bf16[32,2,480,128]{3,1,2,0:T(2,128)(2,1)}), bf16[32,2,480,128]{3,1,2,0:T(2,128)(2,1)}, u32[]{:S(2)}, u32[]{:S(2)}) %all-to-all-start) | async-done | bytes 7864352 | tf_op jit(solution)/shard_map/all_to_all | solution.py:10
  314.1 9.5 %copy.28 = bf16[32,2,480,128]{3,1,0,2:T(2,128)(2,1)S(1)} copy(bf16[32,2,480,128]{3,1,2,0:T(2,128)(2,1)} %all-to-all-done) | data formatting | bytes 15728640 | tf_op jit(solution)/shard_map/all_to_all | solution.py:10
  323.6 2.2 fusion.36
  326.1 0.9 fusion.3
  (51 shorter events, 4.2 us)
Async XLA Ops:
  6.5 319.5 %copy-start = (bf16[128,128]{1,0:T(8,128)(2,1)S(1)}, bf16[128,128]{1,0:T(8,128)(2,1)}, u32[]{:S(2)}) copy-start(bf16[128,128]{1,0:T(8,128)(2,1)} %param.17) | copy-start | bytes 98308
  6.5 16.9 %copy-start.2 = (bf16[3,3,3,128,128]{4,3,2,1,0:T(8,128)(2,1)S(1)}, bf16[3,3,3,128,128]{4,3,2,1,0:T(8,128)(2,1)}, u32[]{:S(2)}) copy-start(bf16[3,3,3,128,128]{4,3,2,1,0:T(8,128)(2,1)} %param.11) | copy-start | bytes 2654212
  9.6 2.9 collective-permute-start
  12.5 11.4 %collective-permute-start.1 = (bf16[4,1,120,128]{3,2,1,0:T(8,128)(2,1)S(1)}, bf16[4,1,120,128]{3,2,1,0:T(8,128)(2,1)S(1)}, u32[]{:S(2)}, u32[]{:S(2)}) collective-permute-start(bf16[4,1,120,128]{3,2,1,0:T(8,128)(2,1)S(1)} %get-tuple-element.82), channel_id=1, source_target_pairs={{0,1},{1,2},{2,3},{3,4},{4,5},{5,6},{6,7},{7,8},{8,9},{9,10},{10,1... | collective-permute-start | bytes 368648 | tf_op jit(solution)/shard_map/ppermute | solution.py:27
  21.5 12.8 %collective-permute-start.2 = (bf16[4,1,120,128]{3,2,1,0:T(8,128)(2,1)S(1)}, bf16[4,1,120,128]{3,2,1,0:T(8,128)(2,1)S(1)}, u32[]{:S(2)}, u32[]{:S(2)}) collective-permute-start(bf16[4,1,120,128]{3,2,1,0:T(8,128)(2,1)S(1)} %get-tuple-element.83), channel_id=1, source_target_pairs={{1,0},{2,1},{3,2},{4,3},{5,4},{6,5},{7,6},{8,7},{9,8},{10,9},{11,1... | collective-permute-start | bytes 368648 | tf_op jit(solution)/shard_map/ppermute | solution.py:28
  39.3 11.9 %copy-start.3 = (bf16[3,3,3,128,128]{4,3,2,1,0:T(8,128)(2,1)S(1)}, bf16[3,3,3,128,128]{4,3,2,1,0:T(8,128)(2,1)}, u32[]{:S(2)}) copy-start(bf16[3,3,3,128,128]{4,3,2,1,0:T(8,128)(2,1)} %param.12) | copy-start | bytes 2654212
  39.7 11.6 %copy-start.7 = (bf16[128]{0:T(256)(128)(2,1)S(1)}, bf16[128]{0:T(256)(128)(2,1)}, u32[]{:S(2)}) copy-start(bf16[128]{0:T(256)(128)(2,1)} %param.13) | copy-start | bytes 772
  39.9 5.5 %collective-permute-start.3 = (bf16[2,4,120,128]{3,2,1,0:T(8,128)(2,1)S(1)}, bf16[2,4,120,128]{3,2,1,0:T(8,128)(2,1)S(1)}, u32[]{:S(2)}, u32[]{:S(2)}) collective-permute-start(bf16[2,4,120,128]{3,2,1,0:T(8,128)(2,1)S(1)} %multiply_convert_fusion.1), channel_id=1, source_target_pairs={{0,16},{16,32},{32,48},{48,64},{64,80},{80,96},{96,112},{112,128},... | collective-permute-start | bytes 737288 | tf_op jit(solution)/shard_map/ppermute | solution.py:17
  45.4 6.8 %collective-permute-start.4 = (bf16[4,1,120,128]{3,2,1,0:T(8,128)(2,1)S(1)}, bf16[4,1,120,128]{3,2,1,0:T(8,128)(2,1)S(1)}, u32[]{:S(2)}, u32[]{:S(2)}) collective-permute-start(bf16[4,1,120,128]{3,2,1,0:T(8,128)(2,1)S(1)} %get-tuple-element.78), channel_id=1, source_target_pairs={{0,1},{1,2},{2,3},{3,4},{4,5},{5,6},{6,7},{7,8},{8,9},{9,10},{10,1... | collective-permute-start | bytes 368648 | tf_op jit(solution)/shard_map/ppermute | solution.py:27
  47.3 12.8 %collective-permute-start.5 = (bf16[4,1,120,128]{3,2,1,0:T(8,128)(2,1)S(1)}, bf16[4,1,120,128]{3,2,1,0:T(8,128)(2,1)S(1)}, u32[]{:S(2)}, u32[]{:S(2)}) collective-permute-start(bf16[4,1,120,128]{3,2,1,0:T(8,128)(2,1)S(1)} %get-tuple-element.79), channel_id=1, source_target_pairs={{1,0},{2,1},{3,2},{4,3},{5,4},{6,5},{7,6},{8,7},{9,8},{10,9},{11,1... | collective-permute-start | bytes 368648 | tf_op jit(solution)/shard_map/ppermute | solution.py:28
  64.7 0.9 copy-start.1
  65.1 1.0 copy-start.4
  65.1 1.0 copy-start.5
  65.1 1.0 copy-start.6
  75.7 238.4 %all-to-all-start = ((bf16[32,2,480,128]{3,1,2,0:T(2,128)(2,1)}), bf16[32,2,480,128]{3,1,2,0:T(2,128)(2,1)}, u32[]{:S(2)}, u32[]{:S(2)}) async-start(bf16[32,2,480,128]{3,1,2,0:T(2,128)(2,1)} %stack.3), calls=%async_computation | async-start | bytes 15728640 | tf_op jit(solution)/shard_map/all_to_all | solution.py:10
  101.8 177.2 %all-gather.2.cloned.1.call-start = ((), (), s32[]{:S(2)}) async-start(), calls=%async_computation.1 | async-start | bytes 8110080 | tf_op jit(solution)/shard_map/all_gather | solution.py:119
Sparse Core Ops, SparseCore 0:
  104.8 174.1 all-gather.1
